TPU v7x, 32 devices: a whole 2x2x4 slice. The times are simulated.
32 devices in a mesh: row: 4 (over y, x), col: 8 (over z, core).
Axes of the slice: x: 2, y: 2, z: 4, core: 2. Of those that a mesh axis runs over, the one named last changes fastest.
Arguments:
- fingerprints: bfloat16 [8192, 1024], P(('row', 'col')), as said below
- probes: bfloat16 [8192, 256], P(('row', 'col')), may hold values from -6 to 6
Outputs:
- image: float32 [8192, 256], P(('row', 'col'))
Inputs may be any that keep to these rules, and one draw needn't show every extreme that they name: `fingerprints`: every entry is positive.
All inputs are finite; a program needn't handle non-finite values.
Results may differ from a plain program's by a relative error of at most 0.0031.
Values may be sent and summed in bfloat16 or wider, within the bound.
A program may use at most 64 MiB of HBM per device.

v0:
```python
import math
import jax
import jax.numpy as jnp
from jax import lax
from jax.sharding import PartitionSpec as P


def squares(rows_now):
    values = rows_now.astype(jnp.float32)
    return jnp.sum(values * values, axis=1)


def tanimoto(first_rows, second_rows, first_sq, second_sq):
    inner = lax.dot_general(
        first_rows, second_rows, (((1,), (1,)), ((), ())), preferred_element_type=jnp.float32
    )
    kernel = inner / (first_sq[:, None] + second_sq[None, :] - inner)
    return kernel.astype(jnp.bfloat16)


def per_device(fingerprints, probes):
    molecules = fingerprints.shape[0] * lax.axis_size("row") * lax.axis_size("col")
    factor = 1.0 / math.sqrt(molecules)
    column_rows, column_probes = (
        lax.all_gather(fingerprints, "row", axis=0, tiled=True),
        lax.all_gather(probes, "row", axis=0, tiled=True),
    )
    column_sq = squares(column_rows)
    shard_rows = lax.all_gather(fingerprints, "col", axis=0, tiled=True)
    kernel = tanimoto(shard_rows, column_rows, squares(shard_rows), column_sq)
    partial_value = jnp.dot(kernel, column_probes, preferred_element_type=jnp.float32)
    owned = lax.psum_scatter(partial_value, "col", scatter_dimension=0, tiled=True)
    return owned * factor


def solution(mesh):
    return jax.shard_map(
        per_device,
        mesh=mesh,
        in_specs=(P(("row", "col"), None), P(("row", "col"), None)),
        out_specs=P(("row", "col"), None),
        check_vma=False,
    )
```

profile of v0, /device:TPU:0, one launch (start us, length us, event | category | flops | bytes accessed | tf_op | source)
XLA Modules:
  0.0 151.5 jit_solution(15270870452908466009)
XLA Ops:
  6.5 0.0 all-gather.5.cloned.1.call-start
  6.5 0.7 all-gather.5.cloned.1.call-update
  7.3 0.0 all-gather.3.cloned.1.call-start
  7.3 0.7 all-gather.3.cloned.1.call-update
  8.0 0.0 reduce-scatter.2.cloned.1.call-start
  8.1 11.8 %all_gather.11 = bf16[1024,256]{1,0:T(8,128)(2,1)S(1)} all-gather(bf16[256,256]{1,0:T(8,128)(2,1)} %param.3), channel_id=1, replica_groups=mesh['row'=4,'col'=8] {'row'}, dimensions={0}, use_global_device_ids=true | all-gather | bytes 655360 | tf_op jit(solution)/shard_map/all_gather | solution.py:26
  19.9 27.4 %all-gather.5.cloned.1.call-done = bf16[1024,1024]{1,0:T(8,128)(2,1)} async-done(((bf16[256,1024]{1,0:T(8,128)(2,1)}), bf16[1024,1024]{1,0:T(8,128)(2,1)}) %all-gather.5.cloned.1.call-update) | async-done | bytes 2097168 | tf_op jit(solution)/shard_map/all_gather | solution.py:25
  47.2 0.0 copy-start
  47.2 2.2 %multiply_reduce_fusion.1 = f32[1024]{0:T(1024)S(1)} fusion(bf16[1024,1024]{1,0:T(8,128)(2,1)} %all-gather.5.cloned.1.call-done), kind=kLoop, calls=%fused_computation.3 | loop fusion | flops 3144704 | bytes 2101248 | tf_op jit(solution)/shard_map/reduce_sum | solution.py:10
  49.5 46.6 %all-gather.3.cloned.1.call-done = bf16[2048,1024]{1,0:T(8,128)(2,1)} async-done(((bf16[256,1024]{1,0:T(8,128)(2,1)}), bf16[2048,1024]{1,0:T(8,128)(2,1)}) %all-gather.3.cloned.1.call-update) | async-done | bytes 4194320 | tf_op jit(solution)/shard_map/all_gather | solution.py:29
  96.0 3.1 %multiply_reduce_fusion = f32[2048]{0:T(1024)S(1)} fusion(bf16[2048,1024]{1,0:T(8,128)(2,1)} %all-gather.3.cloned.1.call-done), kind=kLoop, calls=%fused_computation.2 | loop fusion | flops 6289408 | bytes 4202496 | tf_op jit(solution)/shard_map/reduce_sum | solution.py:10
  99.1 0.0 copy-done
  99.1 9.4 %fusion.1 = f32[2048,256]{1,0:T(8,128)} fusion(bf16[1024,256]{1,0:T(8,128)(2,1)S(1)} %all_gather.11, f32[1024]{0:T(1024)S(1)} %multiply_reduce_fusion.1, f32[2048]{0:T(1024)S(1)} %multiply_reduce_fusion, bf16[2048,1024]{1,0:T(8,128)(2,1)} %all-gather.3.cloned.1.call-done, bf16[1024,1024]{1,0:T(8,128)(2,1)S(1)} %copy-done), kind=kOutput, calls=%fused_computation.4 | convolution fusion | flops 5377097728 | bytes 8925184 | tf_op jit(solution)/shard_map/dot_general | solution.py:31
  108.5 0.0 reduce-scatter.2.cloned.1.call-update
  108.5 34.8 %reduce-scatter.2.cloned.1.call-done = f32[256,256]{1,0:T(8,128)} async-done(((f32[2048,256]{1,0:T(8,128)}), f32[256,256]{1,0:T(8,128)}) %reduce-scatter.2.cloned.1.call-update) | async-done | bytes 262160 | tf_op jit(solution)/shard_map/reduce_scatter | solution.py:32
  143.3 1.7 %broadcast_multiply_fusion = f32[256,256]{1,0:T(8,128)} fusion(f32[256,256]{1,0:T(8,128)} %reduce-scatter.2.cloned.1.call-done), kind=kLoop, calls=%fused_computation.5 | loop fusion | flops 65536 | bytes 524288 | tf_op jit(solution)/shard_map/mul | solution.py:33
Async XLA Ops:
  6.5 40.7 %all-gather.5.cloned.1.call-start = ((), (), s32[]{:S(2)}) async-start(), calls=%async_computation.2 | async-start | bytes 2621440 | tf_op jit(solution)/shard_map/all_gather | solution.py:25
  7.3 88.8 %all-gather.3.cloned.1.call-start = ((), (), s32[]{:S(2)}) async-start(), calls=%async_computation.1 | async-start | bytes 4718592 | tf_op jit(solution)/shard_map/all_gather | solution.py:29
  8.0 135.3 %reduce-scatter.2.cloned.1.call-start = ((), (), s32[]{:S(2)}) async-start(), calls=%async_computation.3 | async-start | bytes 2359296 | tf_op jit(solution)/shard_map/reduce_scatter | solution.py:32
  47.2 51.9 %copy-start = (bf16[1024,1024]{1,0:T(8,128)(2,1)S(1)}, bf16[1024,1024]{1,0:T(8,128)(2,1)}, u32[]{:S(2)}) copy-start(bf16[1024,1024]{1,0:T(8,128)(2,1)} %all-gather.5.cloned.1.call-done) | copy-start | bytes 6291460
Sparse Core Ops, SparseCore 0:
  9.2 38.0 all-gather.4
  48.8 47.1 all-gather.2
  108.7 34.5 reduce-scatter.1
where the time goes:
time: 152 us; the launch traced here: 151 us
  waiting for transfers between devices  110 us (72%)
  between operations  13.1 us (9%)
  blocking collectives  11.8 us (8%)
  matrix products  9.4 us (6%)
  other arithmetic  6.96 us (5%)
    all_gather x1, waiting for transfers between devices, per_device(): shard_rows = lax.all_gather(fingerprints, 'col', axis=0, tiled=True)  46.6 us
    reduce_scatter x1, waiting for transfers between devices, per_device(): lax.psum_scatter(partial_value, 'col', scatter_dimension=0, tiled=True)  34.8 us
    all_gather x1, waiting for transfers between devices, per_device(): lax.all_gather(fingerprints, 'row', axis=0, tiled=True)  27.4 us
    all_gather x1, blocking collectives, per_device(): lax.all_gather(probes, 'row', axis=0, tiled=True)  11.8 us
    dot_general x1, matrix products, per_device(): jnp.dot(kernel, column_probes, preferred_element_type=jnp.float32)  9.4 us
    reduce_sum x2, other arithmetic, squares(): return jnp.sum(values * values, axis=1)  5.29 us
  transfers between devices with their start and end apart: 3, of which 3 were waited for; matrix products, arithmetic and copies ran while one was open for 1% of the time, Pallas kernels for 0%

commit v1 on v0

--- a/solution.py
+++ b/solution.py
@@ -3,6 +3,18 @@
 import jax.numpy as jnp
 from jax import lax
 from jax.sharding import PartitionSpec as P
+
+
+def doubled_up(x, axis, dim):
+    ways, here = (lax.axis_size(axis), lax.axis_index(axis))
+    grown, reach = (x, 1)
+    while reach < ways:
+        theirs = lax.ppermute(grown, axis, [(d, d ^ reach) for d in range(ways)])
+        mine_first = jnp.concatenate([grown, theirs], axis=dim)
+        theirs_first = jnp.concatenate([theirs, grown], axis=dim)
+        grown = jnp.where(here & reach == 0, mine_first, theirs_first)
+        reach = 2 * reach
+    return grown
 
 
 def squares(rows_now):
@@ -22,7 +34,7 @@
     molecules = fingerprints.shape[0] * lax.axis_size("row") * lax.axis_size("col")
     factor = 1.0 / math.sqrt(molecules)
     column_rows, column_probes = (
-        lax.all_gather(fingerprints, "row", axis=0, tiled=True),
+        doubled_up(fingerprints, "row", 0),
         lax.all_gather(probes, "row", axis=0, tiled=True),
     )
     column_sq = squares(column_rows)

time: 152 us -> 115 us (0.76)
  waiting for transfers between devices: 110 us -> 51.3 us
  blocking collectives: 11.8 us -> 28.4 us
  starting transfers between devices: 0.08 us -> 4.88 us
    all_gather x1, waiting for transfers between devices: 46.6 us -> 3.76 us  [per_device(): shard_rows = lax.all_gather(fingerprints, 'col', axis=0, tiled=True)]
    all_gather x1 -> x0, waiting for transfers between devices: 27.4 us -> none  [per_device(): lax.all_gather(fingerprints, 'row', axis=0, tiled=True)]
    all_gather x1, blocking collectives: 11.8 us -> 28.4 us  [per_device(): lax.all_gather(probes, 'row', axis=0, tiled=True)]
    ppermute x0 -> x2, waiting for transfers between devices: none -> 12.1 us  [doubled_up(): theirs = lax.ppermute(grown, axis, [(d, d ^ reach) for d in range(ways)])]
    ppermute x0 -> x2, starting transfers between devices: none -> 4.84 us  [doubled_up(): theirs = lax.ppermute(grown, axis, [(d, d ^ reach) for d in range(ways)])]
    select_n x0 -> x1, other arithmetic: none -> 1.62 us  [doubled_up(): grown = jnp.where(here & reach == 0, mine_first, theirs_first)]
  transfers between devices with their start and end apart: 3 -> 4, of which waited for: 3 -> 3; matrix products, arithmetic and copies ran while one was open for 1% -> 2% of each run, Pallas kernels for 0% -> 0%
where the time goes in v1:
time: 115 us
  waiting for transfers between devices  51.3 us (45%)
  blocking collectives  28.4 us (25%)
  between operations  13.4 us (12%)
  matrix products  9.53 us (8%)
  other arithmetic  7.12 us (6%)
  starting transfers between devices  4.88 us (4%)
    reduce_scatter x1, waiting for transfers between devices, per_device(): lax.psum_scatter(partial_value, 'col', scatter_dimension=0, tiled=True)  34.7 us
    all_gather x1, blocking collectives, per_device(): lax.all_gather(probes, 'row', axis=0, tiled=True)  28.4 us
    ppermute x2, waiting for transfers between devices, doubled_up(): theirs = lax.ppermute(grown, axis, [(d, d ^ reach) for d in range(ways)])  12.1 us
    dot_general x1, matrix products, per_device(): jnp.dot(kernel, column_probes, preferred_element_type=jnp.float32)  9.53 us
    ppermute x2, starting transfers between devices, doubled_up(): theirs = lax.ppermute(grown, axis, [(d, d ^ reach) for d in range(ways)])  4.84 us
    reduce_sum x2, other arithmetic, squares(): return jnp.sum(values * values, axis=1)  3.82 us
    all_gather x1, waiting for transfers between devices, per_device(): shard_rows = lax.all_gather(fingerprints, 'col', axis=0, tiled=True)  3.76 us
  transfers between devices with their start and end apart: 4, of which 3 were waited for; matrix products, arithmetic and copies ran while one was open for 2% of the time, Pallas kernels for 0%

profile of v1, /device:TPU:0, one launch (start us, length us, event | category | flops | bytes accessed | tf_op | source)
XLA Modules:
  0.0 114.7 jit_solution(3704957874694984958)
XLA Ops:
  6.5 0.0 all-gather.2.cloned.1.call-start
  6.5 0.7 all-gather.2.cloned.1.call-update
  7.3 0.0 reduce-scatter.2.cloned.1.call-start
  7.3 3.0 %collective-permute-start = (bf16[256,1024]{1,0:T(8,128)(2,1)}, bf16[256,1024]{1,0:T(8,128)(2,1)S(1)}, u32[]{:S(2)}, u32[]{:S(2)}) collective-permute-start(bf16[256,1024]{1,0:T(8,128)(2,1)} %param.2), channel_id=1, source_target_pairs={{0,8},{8,0},{16,24},{24,16},{1,9},{9,1},{17,25},{25,17},{2,10},{10... | collective-permute-start | bytes 1572872 | tf_op jit(solution)/shard_map/ppermute | solution.py:12
  10.3 12.1 %collective-permute-done = bf16[256,1024]{1,0:T(8,128)(2,1)S(1)} collective-permute-done((bf16[256,1024]{1,0:T(8,128)(2,1)}, bf16[256,1024]{1,0:T(8,128)(2,1)S(1)}, u32[]{:S(2)}, u32[]{:S(2)}) %collective-permute-start) | collective-permute-done | bytes 524320 | tf_op jit(solution)/shard_map/ppermute | solution.py:12
  22.4 1.6 %maximum_select_fusion.1 = bf16[512,1024]{1,0:T(8,128)(2,1)S(1)} fusion(bf16[256,1024]{1,0:T(8,128)(2,1)S(1)} %collective-permute-done, bf16[256,1024]{1,0:T(8,128)(2,1)} %param.2, pred[]{:T(512)S(6)} %eq.7), kind=kLoop, calls=%fused_computation.6 | loop fusion | flops 4718592 | bytes 2097153 | tf_op jit(solution)/shard_map/jit(_where)/select_n | solution.py:15
  24.1 1.8 %collective-permute-start.1 = (bf16[512,1024]{1,0:T(8,128)(2,1)S(1)}, bf16[512,1024]{1,0:T(8,128)(2,1)S(1)}, u32[]{:S(2)}, u32[]{:S(2)}) collective-permute-start(bf16[512,1024]{1,0:T(8,128)(2,1)S(1)} %maximum_select_fusion.1), channel_id=1, source_target_pairs={{0,16},{8,24},{16,0},{24,8},{1,17},{9,25},{17,1},{25,9},{2,18},{10... | collective-permute-start | bytes 3145736 | tf_op jit(solution)/shard_map/ppermute | solution.py:12
  25.9 28.4 %all_gather.7 = bf16[1024,256]{1,0:T(8,128)(2,1)S(1)} all-gather(bf16[256,256]{1,0:T(8,128)(2,1)} %param.3), channel_id=1, replica_groups=mesh['row'=4,'col'=8] {'row'}, dimensions={0}, use_global_device_ids=true | all-gather | bytes 655360 | tf_op jit(solution)/shard_map/all_gather | solution.py:38
  54.3 0.0 collective-permute-done.1
  54.3 0.7 multiply_reduce_fusion.1
  55.1 3.8 %all-gather.2.cloned.1.call-done = bf16[2048,1024]{1,0:T(8,128)(2,1)} async-done(((bf16[256,1024]{1,0:T(8,128)(2,1)}), bf16[2048,1024]{1,0:T(8,128)(2,1)}) %all-gather.2.cloned.1.call-update) | async-done | bytes 4194320 | tf_op jit(solution)/shard_map/all_gather | solution.py:41
  58.8 3.1 %multiply_reduce_fusion = f32[2048]{0:T(1024)S(1)} fusion(bf16[2048,1024]{1,0:T(8,128)(2,1)} %all-gather.2.cloned.1.call-done), kind=kLoop, calls=%fused_computation.2 | loop fusion | flops 6289408 | bytes 4202496 | tf_op jit(solution)/shard_map/reduce_sum | solution.py:22
  61.9 9.5 %fusion.1 = f32[2048,256]{1,0:T(8,128)} fusion(bf16[1024,256]{1,0:T(8,128)(2,1)S(1)} %all_gather.7, bf16[2048,1024]{1,0:T(8,128)(2,1)} %all-gather.2.cloned.1.call-done, f32[1024]{0:T(1024)S(1)} %multiply_reduce_fusion.1, f32[2048]{0:T(1024)S(1)} %multiply_reduce_fusion, bf16[512,1024]{1,0:T(8,128)(2,1)S(1)} %collective-permute-done.1, ...), kind=kOutput, calls=%fused_computation.5 | convolution fusion | flops 5386534912 | bytes 8925185 | tf_op jit(solution)/shard_map/dot_general | solution.py:43
  71.4 0.0 reduce-scatter.2.cloned.1.call-update
  71.5 34.7 %reduce-scatter.2.cloned.1.call-done = f32[256,256]{1,0:T(8,128)} async-done(((f32[2048,256]{1,0:T(8,128)}), f32[256,256]{1,0:T(8,128)}) %reduce-scatter.2.cloned.1.call-update) | async-done | bytes 262160 | tf_op jit(solution)/shard_map/reduce_scatter | solution.py:44
  106.1 1.7 %broadcast_multiply_fusion = f32[256,256]{1,0:T(8,128)} fusion(f32[256,256]{1,0:T(8,128)} %reduce-scatter.2.cloned.1.call-done), kind=kLoop, calls=%fused_computation.7 | loop fusion | flops 65536 | bytes 524288 | tf_op jit(solution)/shard_map/mul | solution.py:45
Async XLA Ops:
  6.5 52.3 %all-gather.2.cloned.1.call-start = ((), (), s32[]{:S(2)}) async-start(), calls=%async_computation.1 | async-start | bytes 4718592 | tf_op jit(solution)/shard_map/all_gather | solution.py:41
  7.3 98.9 %reduce-scatter.2.cloned.1.call-start = ((), (), s32[]{:S(2)}) async-start(), calls=%async_computation.2 | async-start | bytes 2359296 | tf_op jit(solution)/shard_map/reduce_scatter | solution.py:44
  7.3 15.1 %collective-permute-start = (bf16[256,1024]{1,0:T(8,128)(2,1)}, bf16[256,1024]{1,0:T(8,128)(2,1)S(1)}, u32[]{:S(2)}, u32[]{:S(2)}) collective-permute-start(bf16[256,1024]{1,0:T(8,128)(2,1)} %param.2), channel_id=1, source_target_pairs={{0,8},{8,0},{16,24},{24,16},{1,9},{9,1},{17,25},{25,17},{2,10},{10... | collective-permute-start | bytes 1572872 | tf_op jit(solution)/shard_map/ppermute | solution.py:12
  24.1 30.3 %collective-permute-start.1 = (bf16[512,1024]{1,0:T(8,128)(2,1)S(1)}, bf16[512,1024]{1,0:T(8,128)(2,1)S(1)}, u32[]{:S(2)}, u32[]{:S(2)}) collective-permute-start(bf16[512,1024]{1,0:T(8,128)(2,1)S(1)} %maximum_select_fusion.1), channel_id=1, source_target_pairs={{0,16},{8,24},{16,0},{24,8},{1,17},{9,25},{17,1},{25,9},{2,18},{10... | collective-permute-start | bytes 3145736 | tf_op jit(solution)/shard_map/ppermute | solution.py:12
Sparse Core Ops, SparseCore 0:
  9.0 49.8 all-gather.1
  71.6 34.5 reduce-scatter.1
